TPU v7x, 128 devices: a whole 4x4x4 slice. The times are simulated.
128 devices in a mesh: dom: 4 (over y), blk: 32 (over z, x, core).
Axes of the slice: x: 4, y: 4, z: 4, core: 2. Of those that a mesh axis runs over, the one named last changes fastest.
Arguments:
- state: bfloat16 [4, 32, 4, 16, 128, 128], P('dom', 'blk')
- left_env: bfloat16 [4, 32, 14, 128, 128], P('dom', 'blk'), may hold values from -0.5 to 0.5
- right_env: bfloat16 [4, 32, 14, 128, 128], P('dom', 'blk'), may hold values from -0.5 to 0.5
- mpo: bfloat16 [14, 16, 16], replicated, may hold values from -0.375 to 0.375
- mpo_mask: int32 [14, 16, 16], replicated, may hold values 0 or 1
- offsets: int32 [4, 32, 16], P('dom', 'blk'), may hold values from 0 to 4
- sector_rows: int32 [4, 32], P('dom', 'blk'), may hold values from 32 to 128
Outputs:
- residual: float32 [4, 32, 4, 16, 128, 128], P('dom', 'blk')
- theta: float32 [4, 4], P('dom')
All inputs are finite; a program needn't handle non-finite values.
Results may differ from a plain program's by a relative error of at most 0.0052.
Values may be sent and summed in bfloat16 or wider, within the bound.
A program may use at most 64 MiB of HBM per device.

v0:
```python
import jax
import jax.numpy as jnp
from jax import lax
from jax.sharding import PartitionSpec as P

SPAN = 4


def from_partner(block, axis, stride):
    count = lax.axis_size(axis)
    route = []
    for low in range(count):
        high = low | 1 << stride
        if high != low and high < count:
            route += [(low, high), (high, low)]
    return lax.ppermute(block, axis, route)


def passed_along(value, axis, steps):
    count = lax.axis_size(axis)
    initial, last = (max(0, -steps), min(count, count - steps))
    return lax.ppermute(value, axis, [(source, source + steps) for source in range(initial, last)])


def local(state, left_env, right_env, mpo, mpo_mask, offsets, sector_rows):
    f32 = jnp.float32
    bf16 = jnp.bfloat16
    psi = state[0, 0]
    lenv = left_env[0, 0]
    shifts = offsets[0, 0]
    width = psi.shape[-1]
    positions = lax.iota(jnp.int32, width)
    own_live = (positions < sector_rows[0, 0]).astype(bf16)
    mixing = mpo * mpo_mask.astype(bf16)
    partner = from_partner(right_env[0, 0], "dom", 0)
    env_list = [partner]
    live_list = [own_live]
    for step in range(1, SPAN + 1):
        moved_env, moved_live = passed_along((partner, own_live), "blk", -step)
        env_list.append(moved_env)
        live_list.append(moved_live)
    near_env = jnp.stack(env_list)
    near_live = jnp.stack(live_list)

    def accumulate(index, total):
        env_w = lax.dynamic_index_in_dim(near_env, index, 1, keepdims=False)
        picked = jnp.take(env_w, shifts, axis=0)
        mix_w = lax.dynamic_index_in_dim(mixing, index, 0, keepdims=False)
        left_w = lax.dynamic_index_in_dim(lenv, index, 0, keepdims=False)
        mixed = jnp.einsum("ts,vsij->vtij", mix_w, psi, preferred_element_type=f32).astype(bf16)
        lifted = jnp.einsum("ik,vtkj->vtij", left_w, mixed, preferred_element_type=f32).astype(bf16)
        return total + jnp.einsum("vtik,tkj->vtij", lifted, picked, preferred_element_type=f32)

    product = lax.fori_loop(0, mixing.shape[0], accumulate, jnp.zeros(psi.shape, f32))
    col_live = jnp.take(near_live, shifts, axis=0).astype(f32)
    hpsi = product * own_live.astype(f32)[None, None, :, None] * col_live[None, :, None, :]
    psi_wide = psi.astype(f32)
    numer = jnp.sum(psi_wide * hpsi, axis=(1, 2, 3))
    denom = jnp.sum(psi_wide * psi_wide, axis=(1, 2, 3))
    numer, denom = lax.psum((numer, denom), "blk")
    theta = numer / denom
    residual = hpsi - theta[:, None, None, None] * psi_wide
    return (residual[None, None], theta[None])


def solution(mesh):
    placed = (
        P("dom", "blk", None, None, None, None),
        P("dom", "blk", None, None, None),
        P("dom", "blk", None, None, None),
        P(),
        P(),
        P("dom", "blk", None),
        P("dom", "blk"),
    )
    return jax.shard_map(
        local,
        mesh=mesh,
        in_specs=placed,
        out_specs=(P("dom", "blk", None, None, None, None), P("dom", None)),
        check_vma=False,
    )
```

profile of v0, /device:TPU:1, one launch (start us, length us, event | category | flops | bytes accessed | tf_op | source)
XLA Modules:
  0.0 290.6 jit_solution(7957909265634442495)
XLA Ops:
  1.3 3.3 %collective-permute-start.5 = (bf16[128]{0:T(256)(128)(2,1)S(1)}, bf16[128]{0:T(256)(128)(2,1)S(1)}, u32[]{:S(2)}, u32[]{:S(2)}) collective-permute-start(bf16[128]{0:T(256)(128)(2,1)S(1)} %compare_convert_fusion.1), channel_id=1, source_target_pairs={{1,0},{2,1},{3,2},{4,3},{5,4},{6,5},{7,6},{8,7},{9,8},{10,9},{11,1... | collective-permute-start | bytes 776 | tf_op jit(solution)/shard_map/ppermute | solution.py:22
  15.0 6.1 %collective-permute-done = bf16[14,128,128]{2,1,0:T(8,128)(2,1)S(1)} collective-permute-done((bf16[14,128,128]{2,1,0:T(8,128)(2,1)}, bf16[14,128,128]{2,1,0:T(8,128)(2,1)S(1)}, u32[]{:S(2)}, u32[]{:S(2)}) %collective-permute-start) | collective-permute-done | bytes 458784 | tf_op jit(solution)/shard_map/ppermute | solution.py:16
  27.5 7.2 %collective-permute-done.1 = bf16[14,128,128]{2,1,0:T(8,128)(2,1)S(1)} collective-permute-done((bf16[14,128,128]{2,1,0:T(8,128)(2,1)S(1)}, bf16[14,128,128]{2,1,0:T(8,128)(2,1)S(1)}, u32[]{:S(2)}, u32[]{:S(2)}) %collective-permute-start.1) | collective-permute-done | bytes 458784 | tf_op jit(solution)/shard_map/ppermute | solution.py:22
  34.7 4.2 %collective-permute-done.2 = bf16[14,128,128]{2,1,0:T(8,128)(2,1)S(1)} collective-permute-done((bf16[14,128,128]{2,1,0:T(8,128)(2,1)S(1)}, bf16[14,128,128]{2,1,0:T(8,128)(2,1)S(1)}, u32[]{:S(2)}, u32[]{:S(2)}) %collective-permute-start.2) | collective-permute-done | bytes 458784 | tf_op jit(solution)/shard_map/ppermute | solution.py:22
  41.9 3.8 %collective-permute-done.4 = bf16[14,128,128]{2,1,0:T(8,128)(2,1)S(1)} collective-permute-done((bf16[14,128,128]{2,1,0:T(8,128)(2,1)S(1)}, bf16[14,128,128]{2,1,0:T(8,128)(2,1)S(1)}, u32[]{:S(2)}, u32[]{:S(2)}) %collective-permute-start.4) | collective-permute-done | bytes 458784 | tf_op jit(solution)/shard_map/ppermute | solution.py:22
  47.2 146.4 %while.14 = (s32[]{:T(128)}, f32[4,16,128,128]{2,3,0,1:T(8,128)}, s32[16]{0:T(128)S(1)}, bf16[5,14,128,128]{3,2,0,1:T(8,128)(2,1)}, bf16[14,16,16]{2,1,0:T(8,128...) while((s32[]{:T(128)}, f32[4,16,128,128]{2,3,0,1:T(8,128)}, ...), condition=%wide.region_1.2_spmd.clone, body=%wide.region_0.1_spmd.clone.sunk | while | flops 573834368 | bytes 16622043 | solution.py:54
  51.8 4.5 %bitcast_add_fusion.2 = f32[4,16,128,128]{2,3,0,1:T(8,128)} fusion(f32[4,16,128,128]{2,3,0,1:T(8,128)} %get-tuple-element.222, bf16[16,4,128,128]{3,0,2,1:T(8,128)(2,1)S(1)} %fusion.46, pred[]{:T(512)S(6)} %compare.3, bf16[16,128,128]{2,1,0:T(8,128)(2,1)S(1)} %gather_fusion, pred[16]{0:T(512)(128)(4,1)S(1)} %compare_and_fusion.3, ...), kind=kOutput, calls=%fused_computation.2.clone.1 | convolution fusion | flops 540278784 | bytes 11042837 | tf_op jit(solution)/shard_map/while/body/eval_jaxpr/vtik,tkj->vtij/dot_general | solution.py:52
  60.9 5.9 %bitcast_add_fusion.2 = f32[4,16,128,128]{2,3,0,1:T(8,128)} fusion(f32[4,16,128,128]{2,3,0,1:T(8,128)} %get-tuple-element.222, bf16[16,4,128,128]{3,0,2,1:T(8,128)(2,1)S(1)} %fusion.46, pred[]{:T(512)S(6)} %compare.3, bf16[16,128,128]{2,1,0:T(8,128)(2,1)S(1)} %gather_fusion, pred[16]{0:T(512)(128)(4,1)S(1)} %compare_and_fusion.3, ...), kind=kOutput, calls=%fused_computation.2.clone.1 | convolution fusion | flops 540278784 | bytes 11042837 | tf_op jit(solution)/shard_map/while/body/eval_jaxpr/vtik,tkj->vtij/dot_general | solution.py:52
  71.5 5.9 %bitcast_add_fusion.2 = f32[4,16,128,128]{2,3,0,1:T(8,128)} fusion(f32[4,16,128,128]{2,3,0,1:T(8,128)} %get-tuple-element.222, bf16[16,4,128,128]{3,0,2,1:T(8,128)(2,1)S(1)} %fusion.46, pred[]{:T(512)S(6)} %compare.3, bf16[16,128,128]{2,1,0:T(8,128)(2,1)S(1)} %gather_fusion, pred[16]{0:T(512)(128)(4,1)S(1)} %compare_and_fusion.3, ...), kind=kOutput, calls=%fused_computation.2.clone.1 | convolution fusion | flops 540278784 | bytes 11042837 | tf_op jit(solution)/shard_map/while/body/eval_jaxpr/vtik,tkj->vtij/dot_general | solution.py:52
  82.1 5.9 %bitcast_add_fusion.2 = f32[4,16,128,128]{2,3,0,1:T(8,128)} fusion(f32[4,16,128,128]{2,3,0,1:T(8,128)} %get-tuple-element.222, bf16[16,4,128,128]{3,0,2,1:T(8,128)(2,1)S(1)} %fusion.46, pred[]{:T(512)S(6)} %compare.3, bf16[16,128,128]{2,1,0:T(8,128)(2,1)S(1)} %gather_fusion, pred[16]{0:T(512)(128)(4,1)S(1)} %compare_and_fusion.3, ...), kind=kOutput, calls=%fused_computation.2.clone.1 | convolution fusion | flops 540278784 | bytes 11042837 | tf_op jit(solution)/shard_map/while/body/eval_jaxpr/vtik,tkj->vtij/dot_general | solution.py:52
  92.6 5.9 %bitcast_add_fusion.2 = f32[4,16,128,128]{2,3,0,1:T(8,128)} fusion(f32[4,16,128,128]{2,3,0,1:T(8,128)} %get-tuple-element.222, bf16[16,4,128,128]{3,0,2,1:T(8,128)(2,1)S(1)} %fusion.46, pred[]{:T(512)S(6)} %compare.3, bf16[16,128,128]{2,1,0:T(8,128)(2,1)S(1)} %gather_fusion, pred[16]{0:T(512)(128)(4,1)S(1)} %compare_and_fusion.3, ...), kind=kOutput, calls=%fused_computation.2.clone.1 | convolution fusion | flops 540278784 | bytes 11042837 | tf_op jit(solution)/shard_map/while/body/eval_jaxpr/vtik,tkj->vtij/dot_general | solution.py:52
  103.2 5.9 %bitcast_add_fusion.2 = f32[4,16,128,128]{2,3,0,1:T(8,128)} fusion(f32[4,16,128,128]{2,3,0,1:T(8,128)} %get-tuple-element.222, bf16[16,4,128,128]{3,0,2,1:T(8,128)(2,1)S(1)} %fusion.46, pred[]{:T(512)S(6)} %compare.3, bf16[16,128,128]{2,1,0:T(8,128)(2,1)S(1)} %gather_fusion, pred[16]{0:T(512)(128)(4,1)S(1)} %compare_and_fusion.3, ...), kind=kOutput, calls=%fused_computation.2.clone.1 | convolution fusion | flops 540278784 | bytes 11042837 | tf_op jit(solution)/shard_map/while/body/eval_jaxpr/vtik,tkj->vtij/dot_general | solution.py:52
  113.7 5.9 %bitcast_add_fusion.2 = f32[4,16,128,128]{2,3,0,1:T(8,128)} fusion(f32[4,16,128,128]{2,3,0,1:T(8,128)} %get-tuple-element.222, bf16[16,4,128,128]{3,0,2,1:T(8,128)(2,1)S(1)} %fusion.46, pred[]{:T(512)S(6)} %compare.3, bf16[16,128,128]{2,1,0:T(8,128)(2,1)S(1)} %gather_fusion, pred[16]{0:T(512)(128)(4,1)S(1)} %compare_and_fusion.3, ...), kind=kOutput, calls=%fused_computation.2.clone.1 | convolution fusion | flops 540278784 | bytes 11042837 | tf_op jit(solution)/shard_map/while/body/eval_jaxpr/vtik,tkj->vtij/dot_general | solution.py:52
  124.3 5.9 %bitcast_add_fusion.2 = f32[4,16,128,128]{2,3,0,1:T(8,128)} fusion(f32[4,16,128,128]{2,3,0,1:T(8,128)} %get-tuple-element.222, bf16[16,4,128,128]{3,0,2,1:T(8,128)(2,1)S(1)} %fusion.46, pred[]{:T(512)S(6)} %compare.3, bf16[16,128,128]{2,1,0:T(8,128)(2,1)S(1)} %gather_fusion, pred[16]{0:T(512)(128)(4,1)S(1)} %compare_and_fusion.3, ...), kind=kOutput, calls=%fused_computation.2.clone.1 | convolution fusion | flops 540278784 | bytes 11042837 | tf_op jit(solution)/shard_map/while/body/eval_jaxpr/vtik,tkj->vtij/dot_general | solution.py:52
  134.9 5.9 %bitcast_add_fusion.2 = f32[4,16,128,128]{2,3,0,1:T(8,128)} fusion(f32[4,16,128,128]{2,3,0,1:T(8,128)} %get-tuple-element.222, bf16[16,4,128,128]{3,0,2,1:T(8,128)(2,1)S(1)} %fusion.46, pred[]{:T(512)S(6)} %compare.3, bf16[16,128,128]{2,1,0:T(8,128)(2,1)S(1)} %gather_fusion, pred[16]{0:T(512)(128)(4,1)S(1)} %compare_and_fusion.3, ...), kind=kOutput, calls=%fused_computation.2.clone.1 | convolution fusion | flops 540278784 | bytes 11042837 | tf_op jit(solution)/shard_map/while/body/eval_jaxpr/vtik,tkj->vtij/dot_general | solution.py:52
  145.4 5.9 %bitcast_add_fusion.2 = f32[4,16,128,128]{2,3,0,1:T(8,128)} fusion(f32[4,16,128,128]{2,3,0,1:T(8,128)} %get-tuple-element.222, bf16[16,4,128,128]{3,0,2,1:T(8,128)(2,1)S(1)} %fusion.46, pred[]{:T(512)S(6)} %compare.3, bf16[16,128,128]{2,1,0:T(8,128)(2,1)S(1)} %gather_fusion, pred[16]{0:T(512)(128)(4,1)S(1)} %compare_and_fusion.3, ...), kind=kOutput, calls=%fused_computation.2.clone.1 | convolution fusion | flops 540278784 | bytes 11042837 | tf_op jit(solution)/shard_map/while/body/eval_jaxpr/vtik,tkj->vtij/dot_general | solution.py:52
  156.0 5.9 %bitcast_add_fusion.2 = f32[4,16,128,128]{2,3,0,1:T(8,128)} fusion(f32[4,16,128,128]{2,3,0,1:T(8,128)} %get-tuple-element.222, bf16[16,4,128,128]{3,0,2,1:T(8,128)(2,1)S(1)} %fusion.46, pred[]{:T(512)S(6)} %compare.3, bf16[16,128,128]{2,1,0:T(8,128)(2,1)S(1)} %gather_fusion, pred[16]{0:T(512)(128)(4,1)S(1)} %compare_and_fusion.3, ...), kind=kOutput, calls=%fused_computation.2.clone.1 | convolution fusion | flops 540278784 | bytes 11042837 | tf_op jit(solution)/shard_map/while/body/eval_jaxpr/vtik,tkj->vtij/dot_general | solution.py:52
  166.5 5.9 %bitcast_add_fusion.2 = f32[4,16,128,128]{2,3,0,1:T(8,128)} fusion(f32[4,16,128,128]{2,3,0,1:T(8,128)} %get-tuple-element.222, bf16[16,4,128,128]{3,0,2,1:T(8,128)(2,1)S(1)} %fusion.46, pred[]{:T(512)S(6)} %compare.3, bf16[16,128,128]{2,1,0:T(8,128)(2,1)S(1)} %gather_fusion, pred[16]{0:T(512)(128)(4,1)S(1)} %compare_and_fusion.3, ...), kind=kOutput, calls=%fused_computation.2.clone.1 | convolution fusion | flops 540278784 | bytes 11042837 | tf_op jit(solution)/shard_map/while/body/eval_jaxpr/vtik,tkj->vtij/dot_general | solution.py:52
  177.1 5.9 %bitcast_add_fusion.2 = f32[4,16,128,128]{2,3,0,1:T(8,128)} fusion(f32[4,16,128,128]{2,3,0,1:T(8,128)} %get-tuple-element.222, bf16[16,4,128,128]{3,0,2,1:T(8,128)(2,1)S(1)} %fusion.46, pred[]{:T(512)S(6)} %compare.3, bf16[16,128,128]{2,1,0:T(8,128)(2,1)S(1)} %gather_fusion, pred[16]{0:T(512)(128)(4,1)S(1)} %compare_and_fusion.3, ...), kind=kOutput, calls=%fused_computation.2.clone.1 | convolution fusion | flops 540278784 | bytes 11042837 | tf_op jit(solution)/shard_map/while/body/eval_jaxpr/vtik,tkj->vtij/dot_general | solution.py:52
  187.7 5.9 %bitcast_add_fusion.2 = f32[4,16,128,128]{2,3,0,1:T(8,128)} fusion(f32[4,16,128,128]{2,3,0,1:T(8,128)} %get-tuple-element.222, bf16[16,4,128,128]{3,0,2,1:T(8,128)(2,1)S(1)} %fusion.46, pred[]{:T(512)S(6)} %compare.3, bf16[16,128,128]{2,1,0:T(8,128)(2,1)S(1)} %gather_fusion, pred[16]{0:T(512)(128)(4,1)S(1)} %compare_and_fusion.3, ...), kind=kOutput, calls=%fused_computation.2.clone.1 | convolution fusion | flops 540278784 | bytes 11042837 | tf_op jit(solution)/shard_map/while/body/eval_jaxpr/vtik,tkj->vtij/dot_general | solution.py:52
  193.6 5.5 %copy.15 = f32[4,16,128,128]{3,2,1,0:T(8,128)} copy(f32[4,16,128,128]{2,3,0,1:T(8,128)} %get-tuple-element.126) | data formatting | bytes 8388608 | tf_op jit(solution)/shard_map/while | solution.py:54
  199.1 3.5 %fusion.27 = (f32[4]{0:T(128)S(1)}, f32[4]{0:T(128)S(1)}) fusion(bf16[1,1,4,16,128,128]{5,4,3,2,1,0:T(8,128)(2,1)S(1)} %bitcast.96, f32[16,128]{1,0:T(8,128)S(1)} %select_convert_fusion, f32[4,16,128,128]{3,2,1,0:T(8,128)} %copy.15, f32[128]{0:T(128)S(1)} %fusion.31), kind=kLoop, calls=%fused_computation.31 | loop fusion | flops 7340024 | bytes 6300192 | tf_op jit(solution)/shard_map/reduce_sum | solution.py:59
  202.5 82.8 %all-reduce = (f32[4]{0:T(128)S(1)}, f32[4]{0:T(128)S(1)}) all-reduce(f32[4]{0:T(128)S(1)} %get-tuple-element.152, f32[4]{0:T(128)S(1)} %get-tuple-element.151), channel_id=1, replica_groups=mesh['dom'=4,'blk'=32] {'blk'}, use_global_device_ids=true, to_apply=%region_3.4 | all-reduce | flops 8 | bytes 64 | tf_op jit(solution)/shard_map/psum | solution.py:60
  285.3 5.3 %fusion.29 = f32[1,1,4,16,128,128]{5,4,3,2,1,0:T(8,128)} fusion(f32[4,16,128,128]{3,2,1,0:T(8,128)} %copy.15, f32[4]{0:T(128)S(1)} %div.3, f32[16,128]{1,0:T(8,128)S(1)} %select_convert_fusion, f32[128]{0:T(128)S(1)} %fusion.31, bf16[1,1,4,16,128,128]{5,4,3,2,1,0:T(8,128)(2,1)S(1)} %bitcast.97), kind=kLoop, calls=%fused_computation.33 | loop fusion | flops 5242880 | bytes 10494480 | tf_op jit(solution)/shard_map/broadcast_in_dim | solution.py:63
  (122 shorter events, 85.7 us)
Async XLA Ops:
  1.3 11.0 %collective-permute-start.5 = (bf16[128]{0:T(256)(128)(2,1)S(1)}, bf16[128]{0:T(256)(128)(2,1)S(1)}, u32[]{:S(2)}, u32[]{:S(2)}) collective-permute-start(bf16[128]{0:T(256)(128)(2,1)S(1)} %compare_convert_fusion.1), channel_id=1, source_target_pairs={{1,0},{2,1},{3,2},{4,3},{5,4},{6,5},{7,6},{8,7},{9,8},{10,9},{11,1... | collective-permute-start | bytes 776 | tf_op jit(solution)/shard_map/ppermute | solution.py:22
  4.6 7.7 %collective-permute-start.6 = (bf16[128]{0:T(256)(128)(2,1)S(1)}, bf16[128]{0:T(256)(128)(2,1)S(1)}, u32[]{:S(2)}, u32[]{:S(2)}) collective-permute-start(bf16[128]{0:T(256)(128)(2,1)S(1)} %compare_convert_fusion.1), channel_id=1, source_target_pairs={{2,0},{3,1},{4,2},{5,3},{6,4},{7,5},{8,6},{9,7},{10,8},{11,9},{12,... | collective-permute-start | bytes 776 | tf_op jit(solution)/shard_map/ppermute | solution.py:22
  5.9 7.0 %collective-permute-start.7 = (bf16[128]{0:T(256)(128)(2,1)S(1)}, bf16[128]{0:T(256)(128)(2,1)S(1)}, u32[]{:S(2)}, u32[]{:S(2)}) collective-permute-start(bf16[128]{0:T(256)(128)(2,1)S(1)} %compare_convert_fusion.1), channel_id=1, source_target_pairs={{3,0},{4,1},{5,2},{6,3},{7,4},{8,5},{9,6},{10,7},{11,8},{12,9},{13... | collective-permute-start | bytes 776 | tf_op jit(solution)/shard_map/ppermute | solution.py:22
  7.2 7.2 %collective-permute-start.8 = (bf16[128]{0:T(256)(128)(2,1)S(1)}, bf16[128]{0:T(256)(128)(2,1)S(1)}, u32[]{:S(2)}, u32[]{:S(2)}) collective-permute-start(bf16[128]{0:T(256)(128)(2,1)S(1)} %compare_convert_fusion.1), channel_id=1, source_target_pairs={{4,0},{5,1},{6,2},{7,3},{8,4},{9,5},{10,6},{11,7},{12,8},{13,9},{1... | collective-permute-start | bytes 776 | tf_op jit(solution)/shard_map/ppermute | solution.py:22
  8.5 12.5 %collective-permute-start = (bf16[14,128,128]{2,1,0:T(8,128)(2,1)}, bf16[14,128,128]{2,1,0:T(8,128)(2,1)S(1)}, u32[]{:S(2)}, u32[]{:S(2)}) collective-permute-start(bf16[14,128,128]{2,1,0:T(8,128)(2,1)} %bitcast.104), channel_id=1, source_target_pairs={{0,32},{32,0},{64,96},{96,64},{1,33},{33,1},{65,97},{97,65},{2,34}... | collective-permute-start | bytes 1376264 | tf_op jit(solution)/shard_map/ppermute | solution.py:16
  21.0 13.6 %collective-permute-start.1 = (bf16[14,128,128]{2,1,0:T(8,128)(2,1)S(1)}, bf16[14,128,128]{2,1,0:T(8,128)(2,1)S(1)}, u32[]{:S(2)}, u32[]{:S(2)}) collective-permute-start(bf16[14,128,128]{2,1,0:T(8,128)(2,1)S(1)} %collective-permute-done), channel_id=1, source_target_pairs={{1,0},{2,1},{3,2},{4,3},{5,4},{6,5},{7,6},{8,7},{9,8},{10,9},{11,1... | collective-permute-start | bytes 1376264 | tf_op jit(solution)/shard_map/ppermute | solution.py:22
  23.4 23.8 %copy-start.3 = (s32[1,1,16]{2,1,0:T(1,128)S(1)}, s32[1,1,16]{2,1,0:T(1,128)}, u32[]{:S(2)}) copy-start(s32[1,1,16]{2,1,0:T(1,128)} %param.14) | copy-start | bytes 196
  23.4 15.6 %collective-permute-start.2 = (bf16[14,128,128]{2,1,0:T(8,128)(2,1)S(1)}, bf16[14,128,128]{2,1,0:T(8,128)(2,1)S(1)}, u32[]{:S(2)}, u32[]{:S(2)}) collective-permute-start(bf16[14,128,128]{2,1,0:T(8,128)(2,1)S(1)} %collective-permute-done), channel_id=1, source_target_pairs={{2,0},{3,1},{4,2},{5,3},{6,4},{7,5},{8,6},{9,7},{10,8},{11,9},{12,... | collective-permute-start | bytes 1376264 | tf_op jit(solution)/shard_map/ppermute | solution.py:22
  24.8 17.0 %collective-permute-start.3 = (bf16[14,128,128]{2,1,0:T(8,128)(2,1)S(1)}, bf16[14,128,128]{2,1,0:T(8,128)(2,1)S(1)}, u32[]{:S(2)}, u32[]{:S(2)}) collective-permute-start(bf16[14,128,128]{2,1,0:T(8,128)(2,1)S(1)} %collective-permute-done), channel_id=1, source_target_pairs={{3,0},{4,1},{5,2},{6,3},{7,4},{8,5},{9,6},{10,7},{11,8},{12,9},{13... | collective-permute-start | bytes 1376264 | tf_op jit(solution)/shard_map/ppermute | solution.py:22
  26.1 19.6 %collective-permute-start.4 = (bf16[14,128,128]{2,1,0:T(8,128)(2,1)S(1)}, bf16[14,128,128]{2,1,0:T(8,128)(2,1)S(1)}, u32[]{:S(2)}, u32[]{:S(2)}) collective-permute-start(bf16[14,128,128]{2,1,0:T(8,128)(2,1)S(1)} %collective-permute-done), channel_id=1, source_target_pairs={{4,0},{5,1},{6,2},{7,3},{8,4},{9,5},{10,6},{11,7},{12,8},{13,9},{1... | collective-permute-start | bytes 1376264 | tf_op jit(solution)/shard_map/ppermute | solution.py:22
  45.8 1.4 copy-start.1
  193.6 5.5 %copy-start = (bf16[4,16,128,128]{3,2,1,0:T(8,128)(2,1)S(1)}, bf16[4,16,128,128]{3,2,1,0:T(8,128)(2,1)}, u32[]{:S(2)}) copy-start(bf16[4,16,128,128]{3,2,1,0:T(8,128)(2,1)} %get-tuple-element.239) | copy-start | bytes 6291460
  285.3 5.3 %copy-start.2 = (f32[4]{0:T(128)}, f32[4]{0:T(128)S(1)}, u32[]{:S(2)}) copy-start(f32[4]{0:T(128)S(1)} %div.3) | copy-start | bytes 52
where the time goes:
time: 293 us; the launch traced here: 291 us
  matrix products  123 us (42%)
  blocking collectives  82.8 us (28%)
  local copies, waits for them, and re-layouts  29.9 us (10%)
  waiting for transfers between devices  26.2 us (9%)
  starting transfers between devices  15 us (5%)
  other arithmetic  11.4 us (4%)
    psum x1, blocking collectives, local(): numer, denom = lax.psum((numer, denom), 'blk')  82.8 us
    dot_general x14, matrix products, accumulate(): jnp.einsum('vtik,tkj->vtij', lifted, picked, preferred_element_type=f32)  81.2 us
    dot_general x14, matrix products, accumulate(): jnp.einsum('ts,vsij->vtij', mix_w, psi, preferred_element_type=f32)  42.1 us
    ppermute x8, waiting for transfers between devices, passed_along(): lax.ppermute(value, axis, [(source, source + steps) for source in range(i...  20.1 us
    ppermute x8, starting transfers between devices, passed_along(): lax.ppermute(value, axis, [(source, source + steps) for source in range(i...  13.5 us
    squeeze x14, local copies, waits for them, and re-layouts, accumulate(): env_w = lax.dynamic_index_in_dim(near_env, index, 1, keepdims=False)  13.1 us
    gather x14, local copies, waits for them, and re-layouts, accumulate(): picked = jnp.take(env_w, shifts, axis=0)  9.07 us
    ppermute x1, waiting for transfers between devices, from_partner(): return lax.ppermute(block, axis, route)  6.05 us
  transfers between devices with their start and end apart: 9, of which 7 were waited for; matrix products, arithmetic and copies ran while one was open for 1% of the time, Pallas kernels for 0%

commit v1 on v0

v1 whole, which is shorter than its diff:
```python
import jax
import jax.numpy as jnp
from jax import lax
from jax.experimental import pallas as pl
from jax.experimental.pallas import tpu as pltpu
from jax.sharding import PartitionSpec as P

MESH = pl.DeviceIdType.MESH
F32 = jnp.float32
BF16 = jnp.bfloat16

BS = 128
S = 16
W = 14
NV = 4
NEAR = 5
SUB = 16
PIECES = BS // SUB
PAIRS = W // 2
CHUNK = 2
CHUNKS = W // CHUNK
FIRST = 4
SPLIT = FIRST * CHUNK
HEAD = SPLIT * BS
REST = (W - SPLIT) * BS


def remote(src, dst, send, recv, device):
    return pltpu.make_async_remote_copy(
        src_ref=src, dst_ref=dst, send_sem=send, recv_sem=recv, device_id=device, device_id_type=MESH
    )


def apply_kernel(
    n_blk,
    state_ref,
    left_ref,
    right_ref,
    mpo_ref,
    mask_ref,
    offsets_ref,
    rows_ref,
    hpsi_ref,
    psi_ref,
    theta_ref,
    left,
    right,
    own,
    near_a,
    near_b,
    psi_t,
    kron,
    pairs,
    lifted,
    total,
    numer,
    denom,
    sums,
    load_sem,
    send_sem,
    recv_sem,
    sum_send,
    sum_recv,
    known,
):
    dom = lax.axis_index("dom")
    blk = lax.axis_index("blk")
    side = lax.rem(blk, 2)
    partner = (dom + 1 - 2 * lax.rem(dom, 2), blk)
    sibling = (dom, blk + 1 - 2 * side)

    def ring(step):
        return (dom, lax.rem(blk + step + n_blk, n_blk))

    barrier = pltpu.get_barrier_semaphore()
    greeted = [partner] + [ring(step) for step in (1, -1, 2, -2, 4, -4)]
    for device in greeted:
        pl.semaphore_signal(barrier, inc=1, device_id=device, device_id_type=MESH)

    load_right = pltpu.make_async_copy(right_ref, right, load_sem.at[0])
    load_left = pltpu.make_async_copy(left_ref, left, load_sem.at[1])
    load_state = pltpu.make_async_copy(state_ref, psi_ref, load_sem.at[2])
    load_right.start()
    load_state.start()
    load_left.start()

    live = rows_ref[0, 0]
    near_b[0, pl.ds(REST, SUB), :] = jnp.full((SUB, BS), live.astype(F32), F32).astype(BF16)

    has2 = blk < n_blk - 2
    has4 = blk < n_blk - 4
    give2 = blk >= 2
    give4 = blk >= 4

    @pl.when(jnp.logical_not(has2))
    def _():
        near_a[2] = jnp.zeros(near_a.shape[1:], BF16)
        near_b[2] = jnp.zeros(near_b.shape[1:], BF16)

    @pl.when(jnp.logical_not(has4))
    def _():
        near_a[4] = jnp.zeros(near_a.shape[1:], BF16)
        near_b[4] = jnp.zeros(near_b.shape[1:], BF16)

    load_right.wait()
    for w in range(W):
        own[w] = right[w].T

    pl.semaphore_wait(barrier, len(greeted))

    def part(flow, chunk):
        ref, at = (near_a, chunk) if chunk < FIRST else (near_b, chunk - FIRST)
        return ref.at[flow, pl.ds(at * CHUNK * BS, CHUNK * BS), :]

    def copy(src, flow, chunk, device):
        return remote(src, part(flow, chunk), send_sem.at[flow, chunk], recv_sem.at[flow, chunk], device)

    def across(chunk):
        src = own.at[pl.ds(chunk * CHUNK, CHUNK), :, :]
        return remote(
            src,
            part(0, chunk).reshape(CHUNK, BS, BS),
            send_sem.at[0, chunk],
            recv_sem.at[0, chunk],
            partner,
        )

    def by_two(chunk):
        return copy(part(0, chunk), 2, chunk, (dom, blk - 2))

    def by_four(chunk):
        return copy(part(0, chunk), 4, chunk, (dom, blk - 4))

    def beside(flow, chunk):
        return copy(part(flow + 1 - 2 * side, chunk), flow, chunk, sibling)

    def tail(flow):
        return near_b.at[flow, pl.ds(REST, SUB), :]

    def tail_copy(src_flow, flow, device):
        return remote(tail(src_flow), tail(flow), send_sem.at[flow, CHUNKS], recv_sem.at[flow, CHUNKS], device)

    def tail_two():
        return tail_copy(0, 2, (dom, blk - 2))

    def tail_four():
        return tail_copy(0, 4, (dom, blk - 4))

    def tail_beside(flow):
        return tail_copy(flow + 1 - 2 * side, flow, sibling)

    for chunk in range(CHUNKS):
        across(chunk).start()

    @pl.when(give2)
    def _():
        tail_two().start()

    @pl.when(give4)
    def _():
        tail_four().start()

    mixing = (mpo_ref[...] * mask_ref[...].astype(BF16)).reshape(W * S, S)
    spread = (
        lax.broadcasted_iota(jnp.int32, (S, S * SUB), 0) == lax.broadcasted_iota(jnp.int32, (S, S * SUB), 1) // SUB
    )
    spread = spread.astype(F32).astype(BF16)
    spread_t = (
        lax.broadcasted_iota(jnp.int32, (S * SUB, S), 1) == lax.broadcasted_iota(jnp.int32, (S * SUB, S), 0) // SUB
    )
    spread_t = spread_t.astype(F32).astype(BF16)
    wide = jnp.dot(mixing, spread, preferred_element_type=F32).astype(BF16)
    same = lax.rem(lax.broadcasted_iota(jnp.int32, (S * SUB, S * SUB), 0), SUB) == lax.rem(
        lax.broadcasted_iota(jnp.int32, (S * SUB, S * SUB), 1), SUB
    )
    for w in range(W):
        tall = jnp.dot(spread_t, wide[w * S : (w + 1) * S], preferred_element_type=F32)
        kron[w] = jnp.where(same, tall, 0.0).astype(BF16)

    load_state.wait()

    @pl.loop(0, S)
    def _(s):
        row = pl.multiple_of(s * SUB, SUB)
        for v in range(NV):
            psi_t[:, pl.ds(row, SUB), v * BS : (v + 1) * BS] = psi_ref[v * S + s].T.reshape(PIECES, SUB, BS)

    load_left.wait()
    pairs[...] = jnp.zeros_like(pairs)
    for pair in range(PAIRS):
        pairs[pair, :BS, :BS] = left[2 * pair].T
        pairs[pair, BS:, BS:] = left[2 * pair + 1].T

    def arrived_across(chunk):
        across(chunk).wait_recv()

        @pl.when(give2)
        def _():
            by_two(chunk).start()

        @pl.when(give4)
        def _():
            by_four(chunk).start()

        @pl.when(side == 1)
        def _():
            beside(1, chunk).start()

    def arrived_two(chunk):
        @pl.when(has2)
        def _():
            by_two(chunk).wait_recv()

        @pl.when(side == 0)
        def _():
            beside(1, chunk).start()

        @pl.when(side == 1)
        def _():
            beside(3, chunk).start()

    def arrived_four(chunk):
        @pl.when(has4)
        def _():
            by_four(chunk).wait_recv()

        @pl.when(side == 0)
        def _():
            beside(3, chunk).start()

    def tails():
        @pl.when(has2)
        def _():
            tail_two().wait_recv()

        @pl.when(has4)
        def _():
            tail_four().wait_recv()

        tail_beside(1).start()
        tail_beside(3).start()

    def greet(index, steps):
        for step in steps:
            pl.semaphore_signal(known.at[index], inc=1, device_id=ring(step), device_id_type=MESH)

    def at_piece(piece):
        @pl.when(piece == 0)
        def _():
            greet(0, (4, -4))

        @pl.when(piece == 1)
        def _():
            arrived_across(0)
            tails()
            pl.semaphore_wait(known.at[0], 2)
            greet(1, (8, -8))

        @pl.when(piece == 2)
        def _():
            arrived_across(1)
            arrived_across(2)
            pl.semaphore_wait(known.at[1], 2)
            greet(2, (16,))

        @pl.when(piece == 3)
        def _():
            arrived_across(3)
            arrived_across(4)
            pl.semaphore_wait(known.at[2], 1)

        @pl.when(piece == 4)
        def _():
            arrived_across(5)
            arrived_across(6)
            arrived_two(0)

        @pl.when(piece == 5)
        def _():
            arrived_two(1)
            arrived_four(0)

        @pl.when(piece == 6)
        def _():
            arrived_two(2)
            arrived_four(1)

        @pl.when(piece == 7)
        def _():
            arrived_two(3)
            arrived_four(2)

    @pl.loop(0, PIECES)
    def _(piece):
        at_piece(piece)
        row = pl.multiple_of(piece * SUB, SUB)
        for pair in range(PAIRS):
            two = kron[pl.ds(2 * pair, 2)].reshape(2 * S * SUB, S * SUB)
            mixed = jnp.dot(two, psi_t[piece], preferred_element_type=F32).astype(BF16)
            half = S * SUB
            lhs = jnp.concatenate(
                [
                    jnp.concatenate(
                        [mixed[:half, v * BS : (v + 1) * BS], mixed[half:, v * BS : (v + 1) * BS]], axis=1
                    )
                    for v in range(NV)
                ],
                axis=0,
            )
            up = jnp.dot(lhs, pairs[pair], preferred_element_type=F32).astype(BF16)
            for v in range(NV):
                for w in range(2):
                    lifted[:, 2 * pair + w, pl.ds(row, SUB), v * BS : (v + 1) * BS] = up[
                        v * half : (v + 1) * half, w * BS : (w + 1) * BS
                    ].reshape(S, SUB, BS)

    def times_right(t, low, high):
        sector = offsets_ref[0, t]
        block = near_a[sector] if low == 0 else near_b[sector, pl.ds(0, REST), :]
        lhs = jnp.concatenate([block[i * BS : (i + 1) * BS] for i in range(high - low)], axis=1)
        rhs = lifted[t, low:high].reshape((high - low) * BS, NV * BS)
        return jnp.dot(lhs, rhs, preferred_element_type=F32)

    arrived_four(3)
    for chunk in range(FIRST):
        beside(1, chunk).wait_recv()
        beside(3, chunk).wait_recv()

    @pl.loop(0, S // 2)
    def _(t):
        @pl.when(t == 2)
        def _():
            arrived_two(4)
            arrived_two(5)
            arrived_four(4)

        @pl.when(t == 6)
        def _():
            arrived_two(6)
            arrived_four(5)

        for i in range(2):
            total[2 * t + i] = times_right(2 * t + i, 0, SPLIT)

    arrived_four(6)
    for chunk in range(FIRST, CHUNKS):
        beside(1, chunk).wait_recv()
        beside(3, chunk).wait_recv()
    tail_beside(1).wait_recv()
    tail_beside(3).wait_recv()

    numer[...] = jnp.zeros_like(numer)
    denom[...] = jnp.zeros_like(denom)
    wide_row = jnp.full((1, NV * BS), live, jnp.int32)
    row_live = lax.rem(lax.broadcasted_iota(jnp.int32, (1, NV * BS), 1), BS) < wide_row
    column = lax.broadcasted_iota(jnp.int32, (BS, BS), 0).astype(F32)

    @pl.loop(0, S // 2)
    def _(t):
        for i in range(2):
            at = 2 * t + i
            product = total[at] + times_right(at, SPLIT, W)
            bound = near_b[offsets_ref[0, at], pl.ds(REST, SUB), :][:1].astype(F32)
            col_live = jnp.concatenate([column < bound] * NV, axis=1)
            hpsi = jnp.where(jnp.logical_and(col_live, row_live), product, 0.0)
            total[at] = hpsi
            row = pl.multiple_of(at * SUB, SUB)
            psi = psi_t[:, pl.ds(row, SUB), :].reshape(BS, NV * BS).astype(F32)
            numer[...] += jnp.sum((psi * hpsi).reshape(BS // 8, 8, NV * BS), axis=0)
            denom[...] += jnp.sum((psi * psi).reshape(BS // 8, 8, NV * BS), axis=0)

    for v in range(NV):
        sums[blk, v : v + 1] = jnp.sum(numer[:, v * BS : (v + 1) * BS], axis=0, keepdims=True)
        sums[blk, NV + v : NV + v + 1] = jnp.sum(denom[:, v * BS : (v + 1) * BS], axis=0, keepdims=True)

    def tell(step):
        to = lax.rem(blk + step, n_blk)
        return remote(sums.at[blk], sums.at[blk], sum_send.at[step], sum_recv.at[blk], (dom, to))

    def hear(step):
        who = lax.rem(blk + step, n_blk)
        return remote(sums.at[who], sums.at[who], sum_send.at[step], sum_recv.at[who], (dom, who))

    for step in range(1, n_blk):
        tell(step).start()

    @pl.loop(0, S)
    def _(t):
        for v in range(NV):
            hpsi_ref[v * S + t] = total[t, :, v * BS : (v + 1) * BS].T

    for step in range(1, n_blk):
        hear(step).wait_recv()
    total_sums = jnp.sum(jnp.sum(sums[...], axis=0), axis=1, keepdims=True)
    theta_ref[...] = jnp.broadcast_to(total_sums[:NV] / total_sums[NV:], theta_ref.shape)

    for step in range(1, n_blk):
        tell(step).wait_send()
    for chunk in range(CHUNKS):
        across(chunk).wait_send()
        beside(1, chunk).wait_send()
        beside(3, chunk).wait_send()
    tail_beside(1).wait_send()
    tail_beside(3).wait_send()

    @pl.when(give2)
    def _():
        for chunk in range(CHUNKS):
            by_two(chunk).wait_send()
        tail_two().wait_send()

    @pl.when(give4)
    def _():
        for chunk in range(CHUNKS):
            by_four(chunk).wait_send()
        tail_four().wait_send()


def residual_kernel(hpsi_ref, psi_ref, theta_ref, out_ref, theta_out, staged, sem):
    def out(step):
        at = pl.ds(step * (NV * S // 16), NV * S // 16)
        return pltpu.make_async_copy(staged.at[at], out_ref.at[at], sem.at[step])

    for step in range(16):
        each = NV * S // 16
        v = step * each // S
        theta = theta_ref[v : v + 1, :]
        for i in range(each):
            at = step * each + i
            staged[at] = hpsi_ref[at] - theta * psi_ref[at].astype(F32)
        out(step).start()
    picked = lax.broadcasted_iota(jnp.int32, (NV, BS), 0) == lax.broadcasted_iota(jnp.int32, (NV, BS), 1)
    flat = jnp.sum(jnp.where(picked, theta_ref[...], 0.0), axis=0, keepdims=True)
    theta_out[...] = flat[:, :NV]
    for step in range(16):
        out(step).wait()


def local(n_blk, state, left_env, right_env, mpo, mpo_mask, offsets, sector_rows):
    anywhere = pl.BlockSpec(memory_space=pl.ANY)
    vmem = pl.BlockSpec(memory_space=pltpu.VMEM)
    smem = pl.BlockSpec(memory_space=pltpu.SMEM)
    dma = pltpu.SemaphoreType.DMA
    hpsi, psi, theta = pl.pallas_call(
        lambda *refs: apply_kernel(n_blk, *refs),
        out_shape=(
            pltpu.VMEM((NV * S, BS, BS), F32),
            pltpu.VMEM((NV * S, BS, BS), BF16),
            pltpu.VMEM((NV, BS), F32),
        ),
        in_specs=[anywhere, anywhere, anywhere, vmem, vmem, smem, smem],
        out_specs=(vmem, vmem, vmem),
        scratch_shapes=[
            pltpu.VMEM((W, BS, BS), BF16),
            pltpu.VMEM((W, BS, BS), BF16),
            pltpu.VMEM((W, BS, BS), BF16),
            pltpu.VMEM((NEAR, HEAD, BS), BF16),
            pltpu.VMEM((NEAR, REST + SUB, BS), BF16),
            pltpu.VMEM((PIECES, S * SUB, NV * BS), BF16),
            pltpu.VMEM((W, S * SUB, S * SUB), BF16),
            pltpu.VMEM((PAIRS, 2 * BS, 2 * BS), BF16),
            pltpu.VMEM((S, W, BS, NV * BS), BF16),
            pltpu.VMEM((S, BS, NV * BS), F32),
            pltpu.VMEM((8, NV * BS), F32),
            pltpu.VMEM((8, NV * BS), F32),
            pltpu.VMEM((n_blk, 8, BS), F32),
            dma((3,)),
            dma((NEAR, CHUNKS + 1)),
            dma((NEAR, CHUNKS + 1)),
            dma((n_blk,)),
            dma((n_blk,)),
            pltpu.SemaphoreType.REGULAR((3,)),
        ],
        compiler_params=pltpu.CompilerParams(
            collective_id=0, has_side_effects=True, vmem_limit_bytes=52 * 2**20
        ),
    )(
        state.reshape(NV * S, BS, BS),
        left_env.reshape(W, BS, BS),
        right_env.reshape(W, BS, BS),
        mpo,
        mpo_mask,
        offsets.reshape(1, S),
        sector_rows,
    )
    residual, theta = pl.pallas_call(
        residual_kernel,
        out_shape=(jax.ShapeDtypeStruct((NV * S, BS, BS), F32), jax.ShapeDtypeStruct((1, NV), F32)),
        in_specs=[vmem, vmem, vmem],
        out_specs=(anywhere, vmem),
        scratch_shapes=[pltpu.VMEM((NV * S, BS, BS), F32), dma((16,))],
        compiler_params=pltpu.CompilerParams(vmem_limit_bytes=24 * 2**20),
    )(hpsi, psi, theta)
    return residual.reshape(1, 1, NV, S, BS, BS), theta


def solution(mesh):
    n_blk = mesh.shape["blk"]
    placed = (
        P("dom", "blk", None, None, None, None),
        P("dom", "blk", None, None, None),
        P("dom", "blk", None, None, None),
        P(),
        P(),
        P("dom", "blk", None),
        P("dom", "blk"),
    )
    return jax.shard_map(
        lambda *args: local(n_blk, *args),
        mesh=mesh,
        in_specs=placed,
        out_specs=(P("dom", "blk", None, None, None, None), P("dom", None)),
        check_vma=False,
    )
```

time: 293 us -> 49.8 us (0.17)
  matrix products: 123 us -> 0 us
  blocking collectives: 82.8 us -> 0 us
  Pallas kernels: 0 us -> 48.3 us
  local copies, waits for them, and re-layouts: 29.9 us -> 0 us
  waiting for transfers between devices: 26.2 us -> 0 us
  starting transfers between devices: 15 us -> 0 us
  other arithmetic: 11.4 us -> 0 us
    dot_general x28 -> x0, matrix products: 123 us -> none  [the longest x14 81.2 us: accumulate(): jnp.einsum('vtik,tkj->vtij', lifted, picked, preferred_element_type=f32)]
    psum x1 -> x0, blocking collectives: 82.8 us -> none  [local(): numer, denom = lax.psum((numer, denom), 'blk')]
    pallas_call x0 -> x2, Pallas kernels: none -> 48.3 us  [the longest x1 45.6 us: local(): pl.pallas_call(lambda *refs: apply_kernel(n_blk, *refs), out_shape=(pltpu...]
    ppermute x9 -> x0, waiting for transfers between devices: 26.2 us -> none  [the longest x8 20.1 us: passed_along(): lax.ppermute(value, axis, [(source, source + steps) for source in range(i...]
    ppermute x9 -> x0, starting transfers between devices: 15 us -> none  [the longest x8 13.5 us: passed_along(): lax.ppermute(value, axis, [(source, source + steps) for source in range(i...]
    squeeze x14 -> x0, local copies, waits for them, and re-layouts: 13.1 us -> none  [accumulate(): env_w = lax.dynamic_index_in_dim(near_env, index, 1, keepdims=False)]
    gather x15 -> x0, local copies, waits for them, and re-layouts: 9.64 us -> none  [the longest x14 9.07 us: accumulate(): picked = jnp.take(env_w, shifts, axis=0)]
    while x1 -> x0, local copies, waits for them, and re-layouts: 5.48 us -> none  [local(): lax.fori_loop(0, mixing.shape[0], accumulate, jnp.zeros(psi.shape, f32))]
  transfers between devices with their start and end apart: 9 -> 0, of which waited for: 7 -> 0; matrix products, arithmetic and copies ran while one was open for 1% -> 0% of each run, Pallas kernels for 0% -> 0%
where the time goes in v1:
time: 49.8 us; the launch traced here: 49.6 us
  Pallas kernels  48.3 us (97%)
  between operations  1.29 us (3%)
    pallas_call x1, Pallas kernels, local(): pl.pallas_call(lambda *refs: apply_kernel(n_blk, *refs), out_shape=(pltpu...  45.6 us
    pallas_call x1, Pallas kernels, local(): pl.pallas_call(residual_kernel, out_shape=(jax.ShapeDtypeStruct((NV * S,...  2.67 us

profile of v1, /device:TPU:1, one launch (start us, length us, event | category | flops | bytes accessed | tf_op | source)
XLA Modules:
  0.0 49.6 jit_solution(12392965926711010038)
XLA Ops:
  1.3 45.6 %shard_map.86 = (f32[64,128,128]{2,1,0:T(8,128)S(1)}, bf16[64,128,128]{2,1,0:T(8,128)(2,1)S(1)}, f32[4,128]{1,0:T(4,128)S(1)}) custom-call(bf16[64,128,128]{2,1,0:T(8,128)(2,1)} %bitcast.5, bf16[14,128,128]{2,1,0:T(8,128)(2,1)} %bitcast.6, bf16[14,128,128]{2,1,0:T(8,128)(2,1)} %bitcast.7, bf16[14,16,16]{2,1,0:T(8,128)(2,1)} %refs_3_.1, ...), custom_call_target="tpu_custom_call" | custom-call | tf_op jit(solution)/shard_map/pallas_call | solution.py:444
  46.9 2.7 %shard_map.87 = (f32[64,128,128]{2,1,0:T(8,128)}, f32[1,4]{1,0:T(1,128)}) custom-call(f32[64,128,128]{2,1,0:T(8,128)S(1)} %get-tuple-element.7.hpsi_ref, bf16[64,128,128]{2,1,0:T(8,128)(2,1)S(1)} %get-tuple-element.8.psi_ref, f32[4,128]{1,0:T(4,128)S(1)} %get-tuple-element.9.theta_ref), custom_call_target="tpu_custom_call" | custom-call | tf_op jit(solution)/shard_map/pallas_call | solution.py:486

commit v2 on v1

v2 whole, which is shorter than its diff:
```python
import jax
import jax.numpy as jnp
from jax import lax
from jax.experimental import pallas as pl
from jax.experimental.pallas import tpu as pltpu
from jax.sharding import PartitionSpec as P

MESH = pl.DeviceIdType.MESH
F32 = jnp.float32
BF16 = jnp.bfloat16

BS = 128
S = 16
W = 14
NV = 4
NEAR = 5
SUB = 16
PIECES = BS // SUB
PAIRS = W // 2
SPANS = ((0, 4), (4, 8), (8, 11), (11, 14))
CHUNKS = len(SPANS)
FIRST = 2
ROW = 8
ALONG_FIRST = (0,)
ALONG_ROWS = SPANS[ALONG_FIRST[-1]][1] * BS
ONWARD = (2,)
WHEN = (
    (12, "across", 1), (14, "along", 0), (19, "across", 2), (25, "across", 3), (30, "along_four", 0), (37, "two", 2),
    (46, "beside_one", 0), (50, "beside_one", FIRST), (55, "beside_three", 0), (60, "beside_three", FIRST),
)
SPLIT = SPANS[FIRST][0]
HEAD = SPLIT * BS
REST = (W - SPLIT) * BS


def remote(src, dst, send, recv, device):
    return pltpu.make_async_remote_copy(
        src_ref=src, dst_ref=dst, send_sem=send, recv_sem=recv, device_id=device, device_id_type=MESH
    )


def apply_kernel(
    n_blk,
    state_ref,
    left_ref,
    right_ref,
    mpo_ref,
    mask_ref,
    offsets_ref,
    rows_ref,
    hpsi_ref,
    psi_ref,
    theta_ref,
    left,
    right,
    mpo,
    mask,
    offsets,
    rows,
    own,
    near_a,
    near_b,
    along_two,
    along_four,
    transit,
    psi_t,
    kron,
    pairs,
    mixed_a,
    mixed_b,
    lifted,
    total,
    numer,
    denom,
    sums,
    load_sem,
    send_sem,
    recv_sem,
    sum_send,
    sum_recv,
    known,
):
    dom = lax.axis_index("dom")
    blk = lax.axis_index("blk")
    side = lax.rem(blk, 2)
    partner = (dom + 1 - 2 * lax.rem(dom, 2), blk)
    sibling = (dom, blk + 1 - 2 * side)

    def ring(step, start=blk):
        return (dom, lax.rem(start + step + n_blk, n_blk))

    def along(step, start=blk):
        place = lax.rem(start, ROW)
        return start - place + lax.rem(place + step + ROW, ROW)

    row_next = (dom, along(2))
    row_last = (dom, along(-2))
    stop = (dom, along(-2, ring(-4)[1]))
    stops_here = ring(4, along(2))

    barrier = pltpu.get_barrier_semaphore()
    greeted = [partner, sibling, row_next, row_last, stop, stops_here]
    greeted += [ring(step) for step in (2, -2, 4, -4)]
    for device in greeted:
        pl.semaphore_signal(barrier, inc=1, device_id=device, device_id_type=MESH)

    load_rows = pltpu.make_async_copy(rows_ref, rows, load_sem.at[0])
    load_right = pltpu.make_async_copy(right_ref, right, load_sem.at[1])
    load_mpo = pltpu.make_async_copy(mpo_ref, mpo, load_sem.at[2])
    load_mask = pltpu.make_async_copy(mask_ref, mask, load_sem.at[3])
    load_state = pltpu.make_async_copy(state_ref, psi_ref, load_sem.at[4])
    load_left = pltpu.make_async_copy(left_ref, left, load_sem.at[5])
    load_offsets = pltpu.make_async_copy(offsets_ref, offsets, load_sem.at[6])
    for load in (load_rows, load_right, load_mpo, load_mask, load_state, load_left, load_offsets):
        load.start()

    load_rows.wait()
    live = rows[0, 0]
    near_b[0, pl.ds(REST, SUB), :] = jnp.full((SUB, BS), live.astype(F32), F32).astype(BF16)

    load_right.wait()
    for w in range(W):
        own[w * BS : (w + 1) * BS] = right[w].T

    pl.semaphore_wait(barrier, len(greeted))

    def part(flow, chunk, count=1):
        ref, base = (near_a, 0) if chunk < FIRST else (near_b, SPLIT)
        low, high = SPANS[chunk][0], SPANS[chunk + count - 1][1]
        return ref.at[flow, pl.ds((low - base) * BS, (high - low) * BS), :]

    def span(ref, chunk):
        low, high = SPANS[chunk]
        return ref.at[pl.ds(low * BS, (high - low) * BS), :]

    def copy(src, dst, flow, chunk, device):
        return remote(src, dst, send_sem.at[flow, chunk], recv_sem.at[flow, chunk], device)

    def mine(chunk):
        return span(own, chunk)

    def across(chunk):
        return copy(mine(chunk), part(0, chunk), 0, chunk, partner)

    def along_by_two(chunk):
        return copy(mine(chunk), span(along_two, chunk), 6, chunk, ring(-2))

    def along_stop(chunk):
        return copy(mine(chunk), span(transit, chunk), 5, chunk, stop)

    def along_by_four(chunk):
        return copy(span(transit, chunk), span(along_four, chunk), 7, chunk, row_next)

    def by_two(chunk):
        if chunk in ALONG_FIRST:
            return copy(span(along_two, chunk), part(2, chunk), 2, chunk, partner)
        return copy(part(0, chunk), part(2, chunk), 2, chunk, ring(-2))

    def by_four(chunk):
        if chunk in ALONG_FIRST:
            return copy(span(along_four, chunk), part(4, chunk), 4, chunk, partner)
        if chunk in ONWARD:
            return copy(part(2, chunk), part(4, chunk), 4, chunk, ring(-2))
        return copy(part(0, chunk), part(4, chunk), 4, chunk, ring(-4))

    def beside(flow, chunk):
        count = FIRST if chunk == 0 else CHUNKS - FIRST
        return copy(part(flow + 1 - 2 * side, chunk, count), part(flow, chunk, count), flow, chunk, sibling)

    def tail(flow):
        return near_b.at[flow, pl.ds(REST, SUB), :]

    def tail_two():
        return copy(tail(0), tail(2), 2, CHUNKS, ring(-2))

    def tail_four():
        return copy(tail(0), tail(4), 4, CHUNKS, ring(-4))

    def tail_beside(flow):
        return copy(tail(flow + 1 - 2 * side), tail(flow), flow, CHUNKS, sibling)

    sent = []

    def send(transfer, *which):
        transfer(*which).start()
        sent.append((transfer, which))

    for chunk in ALONG_FIRST:
        send(along_stop, chunk)
        send(along_by_two, chunk)
    for chunk in range(CHUNKS):
        if chunk not in ALONG_FIRST:
            send(across, chunk)
    for chunk in ALONG_FIRST:
        send(across, chunk)
    send(tail_two)
    send(tail_four)

    load_mpo.wait()
    load_mask.wait()
    mixing = (mpo[...] * mask[...].astype(BF16)).reshape(W * S, S)
    spread = (
        lax.broadcasted_iota(jnp.int32, (S, S * SUB), 0) == lax.broadcasted_iota(jnp.int32, (S, S * SUB), 1) // SUB
    )
    spread = spread.astype(F32).astype(BF16)
    spread_t = (
        lax.broadcasted_iota(jnp.int32, (S * SUB, S), 1) == lax.broadcasted_iota(jnp.int32, (S * SUB, S), 0) // SUB
    )
    spread_t = spread_t.astype(F32).astype(BF16)
    wide = jnp.dot(mixing, spread, preferred_element_type=F32).astype(BF16)
    same = lax.rem(lax.broadcasted_iota(jnp.int32, (S * SUB, S * SUB), 0), SUB) == lax.rem(
        lax.broadcasted_iota(jnp.int32, (S * SUB, S * SUB), 1), SUB
    )
    for w in range(W):
        tall = jnp.dot(spread_t, wide[w * S : (w + 1) * S], preferred_element_type=F32)
        kron[w] = jnp.where(same, tall, 0.0).astype(BF16)

    load_left.wait()
    pairs[...] = jnp.zeros_like(pairs)
    for pair in range(PAIRS):
        pairs[pair, :BS, :BS] = left[2 * pair].T
        pairs[pair, BS:, BS:] = left[2 * pair + 1].T

    load_state.wait()

    @pl.loop(0, S // 2)
    def _(s):
        for i in range(2):
            row = pl.multiple_of((2 * s + i) * SUB, SUB)
            for v in range(NV):
                psi_t[:, pl.ds(row, SUB), v * BS : (v + 1) * BS] = psi_ref[v * S + 2 * s + i].T.reshape(PIECES, SUB, BS)

    def arrived(kind, chunk):
        if kind == "along":
            along_stop(chunk).wait_recv()
            send(along_by_four, chunk)
            along_by_two(chunk).wait_recv()
            send(by_two, chunk)
        elif kind == "along_four":
            along_by_four(chunk).wait_recv()
            send(by_four, chunk)
        elif kind == "across":
            across(chunk).wait_recv()
            send(by_two, chunk)
            if chunk not in ONWARD:
                send(by_four, chunk)
        elif kind == "two":
            by_two(chunk).wait_recv()
            send(by_four, chunk)
        else:
            for at in range(FIRST) if chunk == 0 else range(FIRST, CHUNKS):
                if kind == "beside_three":
                    by_four(at).wait_recv()
                elif at not in ONWARD:
                    by_two(at).wait_recv()
                if kind == "beside_one" and at in ALONG_FIRST:
                    across(at).wait_recv()
            send(beside, 1 if kind == "beside_one" else 3, chunk)

    def tails():
        tail_two().wait_recv()
        tail_four().wait_recv()
        send(tail_beside, 1)
        send(tail_beside, 3)

    def greet(index, steps):
        if index > 0:
            pl.semaphore_wait(known.at[index - 1], 2)
        for step in steps:
            pl.semaphore_signal(known.at[index], inc=1, device_id=ring(step), device_id_type=MESH)

    events = {}

    def plan(step, action):
        events.setdefault(step, []).append(action)

    plan(2, lambda: greet(0, (4, -4)))
    plan(14, lambda: greet(1, (8, -8)))
    plan(26, lambda: greet(2, (16,)))
    plan(38, lambda: pl.semaphore_wait(known.at[2], 1))
    plan(22, tails)
    for at, kind, chunk in WHEN:
        plan(at, lambda kind=kind, chunk=chunk: arrived(kind, chunk))
    steps = PIECES * PAIRS

    def run(step):
        for action in events.pop(step, ()):
            action()

    halves = (mixed_a, mixed_b)
    half = S * SUB

    def mix(step):
        piece, pair = divmod(step, PAIRS)
        two = kron[2 * pair : 2 * pair + 2].reshape(2 * half, half)
        mixed = jnp.dot(two, psi_t[piece], preferred_element_type=F32).astype(BF16)
        to = halves[step % 2]
        for v in range(NV):
            for w in range(2):
                to[v * half : (v + 1) * half, w * BS : (w + 1) * BS] = mixed[
                    w * half : (w + 1) * half, v * BS : (v + 1) * BS
                ]

    def lift(step):
        piece, pair = divmod(step, PAIRS)
        up = jnp.dot(halves[step % 2][...], pairs[pair], preferred_element_type=F32).astype(BF16)
        for v in range(NV):
            for w in range(2):
                lifted[:, 2 * pair + w, piece * SUB : (piece + 1) * SUB, v * BS : (v + 1) * BS] = up[
                    v * half : (v + 1) * half, w * BS : (w + 1) * BS
                ].reshape(S, SUB, BS)

    mix(0)
    for step in range(steps):
        run(step)
        if step + 1 < steps:
            mix(step + 1)
        lift(step)

    load_offsets.wait()

    def times_right(t, low, high):
        sector = offsets[0, t]
        block = near_a[sector] if low == 0 else near_b[sector, pl.ds(0, REST), :]
        lhs = jnp.concatenate([block[i * BS : (i + 1) * BS] for i in range(high - low)], axis=1)
        rhs = lifted[t, low:high].reshape((high - low) * BS, NV * BS)
        return jnp.dot(lhs, rhs, preferred_element_type=F32)

    def psi_of(t):
        row = pl.multiple_of(t * SUB, SUB)
        return psi_t[:, pl.ds(row, SUB), :].reshape(BS, NV * BS).astype(F32)

    run(steps)
    beside(1, 0).wait_recv()
    beside(3, 0).wait_recv()
    numer[...] = jnp.zeros_like(numer)
    denom[...] = jnp.zeros_like(denom)
    late = sorted(events)

    @pl.loop(0, S // 4)
    def _(t):
        for at in late:
            if at - steps < 8:

                @pl.when(t == (at - steps) // 2)
                def _(at=at):
                    run(at)

        for i in range(4):
            total[4 * t + i] = times_right(4 * t + i, 0, SPLIT)
            psi = psi_of(4 * t + i)
            denom[...] += jnp.sum((psi * psi).reshape(BS // 8, 8, NV * BS), axis=0)

    for at in sorted(events):
        run(at)
    beside(1, FIRST).wait_recv()
    beside(3, FIRST).wait_recv()
    tail_beside(1).wait_recv()
    tail_beside(3).wait_recv()

    wide_row = jnp.full((1, NV * BS), live, jnp.int32)
    row_live = lax.rem(lax.broadcasted_iota(jnp.int32, (1, NV * BS), 1), BS) < wide_row
    column = lax.broadcasted_iota(jnp.int32, (BS, BS), 0).astype(F32)

    @pl.loop(0, S // 4)
    def _(t):
        for i in range(4):
            at = 4 * t + i
            product = total[at] + times_right(at, SPLIT, W)
            sector = offsets[0, at]
            bound = near_b[sector, pl.ds(REST, SUB), :][:1].astype(F32)
            bound = jnp.where(jnp.full((1, BS), blk + sector, jnp.int32) < n_blk, bound, 0.0)
            col_live = jnp.concatenate([column < bound] * NV, axis=1)
            hpsi = jnp.where(jnp.logical_and(col_live, row_live), product, 0.0)
            total[at] = hpsi
            numer[...] += jnp.sum((psi_of(at) * hpsi).reshape(BS // 8, 8, NV * BS), axis=0)

    for v in range(NV):
        sums[blk, v : v + 1] = jnp.sum(numer[:, v * BS : (v + 1) * BS], axis=0, keepdims=True)
        sums[blk, NV + v : NV + v + 1] = jnp.sum(denom[:, v * BS : (v + 1) * BS], axis=0, keepdims=True)

    def tell(step):
        to = lax.rem(blk + step, n_blk)
        return remote(sums.at[blk], sums.at[blk], sum_send.at[step], sum_recv.at[blk], (dom, to))

    def hear(step):
        who = lax.rem(blk + step, n_blk)
        return remote(sums.at[who], sums.at[who], sum_send.at[step], sum_recv.at[who], (dom, who))

    for step in range(1, n_blk):
        tell(step).start()

    @pl.loop(0, S // 2)
    def _(t):
        for i in range(2):
            for v in range(NV):
                hpsi_ref[v * S + 2 * t + i] = total[2 * t + i, :, v * BS : (v + 1) * BS].T

    for transfer, which in sent:
        transfer(*which).wait_send()
    for step in range(1, n_blk):
        hear(step).wait_recv()
    total_sums = jnp.sum(jnp.sum(sums[...], axis=0), axis=1, keepdims=True)
    theta_ref[...] = jnp.broadcast_to(total_sums[:NV] / total_sums[NV:], theta_ref.shape)
    for step in range(1, n_blk):
        tell(step).wait_send()


def residual_kernel(hpsi_ref, psi_ref, theta_ref, out_ref, theta_out, staged, sem):
    def out(step):
        at = pl.ds(step * (NV * S // 16), NV * S // 16)
        return pltpu.make_async_copy(staged.at[at], out_ref.at[at], sem.at[step])

    for step in range(16):
        each = NV * S // 16
        v = step * each // S
        theta = theta_ref[v : v + 1, :]
        for i in range(each):
            at = step * each + i
            staged[at] = hpsi_ref[at] - theta * psi_ref[at].astype(F32)
        out(step).start()
    picked = lax.broadcasted_iota(jnp.int32, (NV, BS), 0) == lax.broadcasted_iota(jnp.int32, (NV, BS), 1)
    flat = jnp.sum(jnp.where(picked, theta_ref[...], 0.0), axis=0, keepdims=True)
    theta_out[...] = flat[:, :NV]
    for step in range(16):
        out(step).wait()


def local(n_blk, state, left_env, right_env, mpo, mpo_mask, offsets, sector_rows):
    anywhere = pl.BlockSpec(memory_space=pl.ANY)
    vmem = pl.BlockSpec(memory_space=pltpu.VMEM)
    dma = pltpu.SemaphoreType.DMA
    hpsi, psi, theta = pl.pallas_call(
        lambda *refs: apply_kernel(n_blk, *refs),
        out_shape=(
            pltpu.VMEM((NV * S, BS, BS), F32),
            pltpu.VMEM((NV * S, BS, BS), BF16),
            pltpu.VMEM((NV, BS), F32),
        ),
        in_specs=[anywhere] * 7,
        out_specs=(vmem, vmem, vmem),
        scratch_shapes=[
            pltpu.VMEM((W, BS, BS), BF16),
            pltpu.VMEM((W, BS, BS), BF16),
            pltpu.VMEM((W, S, S), BF16),
            pltpu.VMEM((W, S, S), jnp.int32),
            pltpu.SMEM((1, S), jnp.int32),
            pltpu.SMEM((1, 1), jnp.int32),
            pltpu.VMEM((W * BS, BS), BF16),
            pltpu.VMEM((NEAR, HEAD, BS), BF16),
            pltpu.VMEM((NEAR, REST + SUB, BS), BF16),
            pltpu.VMEM((ALONG_ROWS, BS), BF16),
            pltpu.VMEM((ALONG_ROWS, BS), BF16),
            pltpu.VMEM((ALONG_ROWS, BS), BF16),
            pltpu.VMEM((PIECES, S * SUB, NV * BS), BF16),
            pltpu.VMEM((W, S * SUB, S * SUB), BF16),
            pltpu.VMEM((PAIRS, 2 * BS, 2 * BS), BF16),
            pltpu.VMEM((NV * S * SUB, 2 * BS), BF16),
            pltpu.VMEM((NV * S * SUB, 2 * BS), BF16),
            pltpu.VMEM((S, W, BS, NV * BS), BF16),
            pltpu.VMEM((S, BS, NV * BS), F32),
            pltpu.VMEM((8, NV * BS), F32),
            pltpu.VMEM((8, NV * BS), F32),
            pltpu.VMEM((n_blk, 8, BS), F32),
            dma((7,)),
            dma((NEAR + 3, CHUNKS + 1)),
            dma((NEAR + 3, CHUNKS + 1)),
            dma((n_blk,)),
            dma((n_blk,)),
            pltpu.SemaphoreType.REGULAR((3,)),
        ],
        compiler_params=pltpu.CompilerParams(
            collective_id=0, has_side_effects=True, vmem_limit_bytes=52 * 2**20
        ),
    )(
        state.reshape(NV * S, BS, BS),
        left_env.reshape(W, BS, BS),
        right_env.reshape(W, BS, BS),
        mpo,
        mpo_mask,
        offsets.reshape(1, S),
        sector_rows,
    )
    residual, theta = pl.pallas_call(
        residual_kernel,
        out_shape=(jax.ShapeDtypeStruct((NV * S, BS, BS), F32), jax.ShapeDtypeStruct((1, NV), F32)),
        in_specs=[vmem, vmem, vmem],
        out_specs=(anywhere, vmem),
        scratch_shapes=[pltpu.VMEM((NV * S, BS, BS), F32), dma((16,))],
        compiler_params=pltpu.CompilerParams(vmem_limit_bytes=24 * 2**20),
    )(hpsi, psi, theta)
    return residual.reshape(1, 1, NV, S, BS, BS), theta


def solution(mesh):
    n_blk = mesh.shape["blk"]
    placed = (
        P("dom", "blk", None, None, None, None),
        P("dom", "blk", None, None, None),
        P("dom", "blk", None, None, None),
        P(),
        P(),
        P("dom", "blk", None),
        P("dom", "blk"),
    )
    return jax.shard_map(
        lambda *args: local(n_blk, *args),
        mesh=mesh,
        in_specs=placed,
        out_specs=(P("dom", "blk", None, None, None, None), P("dom", None)),
        check_vma=False,
    )
```

time: 49.8 us -> 47.9 us (0.962)
  Pallas kernels: 48.3 us -> 46.3 us
    pallas_call x1, Pallas kernels: 45.6 us -> 43.6 us  [local(): pl.pallas_call(lambda *refs: apply_kernel(n_blk, *refs), out_shape=(pltpu...]
where the time goes in v2:
time: 47.9 us; the launch traced here: 47.7 us
  Pallas kernels  46.3 us (97%)
  between operations  1.45 us (3%)
    pallas_call x1, Pallas kernels, local(): pl.pallas_call(lambda *refs: apply_kernel(n_blk, *refs), out_shape=(pltpu...  43.6 us
    pallas_call x1, Pallas kernels, local(): pl.pallas_call(residual_kernel, out_shape=(jax.ShapeDtypeStruct((NV * S,...  2.67 us

profile of v2, /device:TPU:1, one launch (start us, length us, event | category | flops | bytes accessed | tf_op | source)
XLA Modules:
  0.0 47.7 jit_solution(3785958913161418477)
XLA Ops:
  1.3 43.6 %shard_map.86 = (f32[64,128,128]{2,1,0:T(8,128)S(1)}, bf16[64,128,128]{2,1,0:T(8,128)(2,1)S(1)}, f32[4,128]{1,0:T(4,128)S(1)}) custom-call(bf16[64,128,128]{2,1,0:T(8,128)(2,1)} %bitcast.5, bf16[14,128,128]{2,1,0:T(8,128)(2,1)} %bitcast.6, bf16[14,128,128]{2,1,0:T(8,128)(2,1)} %bitcast.7, bf16[14,16,16]{2,1,0:T(8,128)(2,1)} %refs_3_.1, ...), custom_call_target="tpu_custom_call" | custom-call | tf_op jit(solution)/shard_map/pallas_call | solution.py:433
  44.9 2.7 %shard_map.87 = (f32[64,128,128]{2,1,0:T(8,128)}, f32[1,4]{1,0:T(1,128)}) custom-call(f32[64,128,128]{2,1,0:T(8,128)S(1)} %get-tuple-element.7.hpsi_ref, bf16[64,128,128]{2,1,0:T(8,128)(2,1)S(1)} %get-tuple-element.8.psi_ref, f32[4,128]{1,0:T(4,128)S(1)} %get-tuple-element.9.theta_ref), custom_call_target="tpu_custom_call" | custom-call | tf_op jit(solution)/shard_map/pallas_call | solution.py:484

commit v3 on v2

--- a/solution.py
+++ b/solution.py
@@ -25,8 +25,8 @@
 ALONG_ROWS = SPANS[ALONG_FIRST[-1]][1] * BS
 ONWARD = (2,)
 WHEN = (
-    (12, "across", 1), (14, "along", 0), (19, "across", 2), (25, "across", 3), (30, "along_four", 0), (37, "two", 2),
-    (46, "beside_one", 0), (50, "beside_one", FIRST), (55, "beside_three", 0), (60, "beside_three", FIRST),
+    (14, "across", 1), (17, "along", 0), (22, "across", 2), (28, "across", 3), (34, "along_four", 0), (42, "two", 2),
+    (50, "beside_one", 0), (53, "beside_one", FIRST), (56, "beside_three", 0), (60, "beside_three", FIRST),
 )
 SPLIT = SPANS[FIRST][0]
 HEAD = SPLIT * BS
@@ -124,10 +124,11 @@
 
     pl.semaphore_wait(barrier, len(greeted))
 
-    def part(flow, chunk, count=1):
+    def part(flow, chunk, count=1, across=False):
         ref, base = (near_a, 0) if chunk < FIRST else (near_b, SPLIT)
         low, high = SPANS[chunk][0], SPANS[chunk + count - 1][1]
-        return ref.at[flow, pl.ds((low - base) * BS, (high - low) * BS), :]
+        behind = SUB if high == W and not across else 0
+        return ref.at[flow, pl.ds((low - base) * BS, (high - low) * BS + behind), :]
 
     def span(ref, chunk):
         low, high = SPANS[chunk]
@@ -140,7 +141,7 @@
         return span(own, chunk)
 
     def across(chunk):
-        return copy(mine(chunk), part(0, chunk), 0, chunk, partner)
+        return copy(mine(chunk), part(0, chunk, across=True), 0, chunk, partner)
 
     def along_by_two(chunk):
         return copy(mine(chunk), span(along_two, chunk), 6, chunk, ring(-2))
@@ -166,18 +167,6 @@
     def beside(flow, chunk):
         count = FIRST if chunk == 0 else CHUNKS - FIRST
         return copy(part(flow + 1 - 2 * side, chunk, count), part(flow, chunk, count), flow, chunk, sibling)
-
-    def tail(flow):
-        return near_b.at[flow, pl.ds(REST, SUB), :]
-
-    def tail_two():
-        return copy(tail(0), tail(2), 2, CHUNKS, ring(-2))
-
-    def tail_four():
-        return copy(tail(0), tail(4), 4, CHUNKS, ring(-4))
-
-    def tail_beside(flow):
-        return copy(tail(flow + 1 - 2 * side), tail(flow), flow, CHUNKS, sibling)
 
     sent = []
 
@@ -193,8 +182,6 @@
             send(across, chunk)
     for chunk in ALONG_FIRST:
         send(across, chunk)
-    send(tail_two)
-    send(tail_four)
 
     load_mpo.wait()
     load_mask.wait()
@@ -257,12 +244,6 @@
                     across(at).wait_recv()
             send(beside, 1 if kind == "beside_one" else 3, chunk)
 
-    def tails():
-        tail_two().wait_recv()
-        tail_four().wait_recv()
-        send(tail_beside, 1)
-        send(tail_beside, 3)
-
     def greet(index, steps):
         if index > 0:
             pl.semaphore_wait(known.at[index - 1], 2)
@@ -278,7 +259,6 @@
     plan(14, lambda: greet(1, (8, -8)))
     plan(26, lambda: greet(2, (16,)))
     plan(38, lambda: pl.semaphore_wait(known.at[2], 1))
-    plan(22, tails)
     for at, kind, chunk in WHEN:
         plan(at, lambda kind=kind, chunk=chunk: arrived(kind, chunk))
     steps = PIECES * PAIRS
@@ -331,10 +311,17 @@
         return psi_t[:, pl.ds(row, SUB), :].reshape(BS, NV * BS).astype(F32)
 
     run(steps)
+    numer[...] = jnp.zeros_like(numer)
+    denom[...] = jnp.zeros_like(denom)
+
+    @pl.loop(0, S // 4)
+    def _(t):
+        for i in range(4):
+            psi = psi_of(4 * t + i)
+            denom[...] += jnp.sum((psi * psi).reshape(BS // 8, 8, NV * BS), axis=0)
+
     beside(1, 0).wait_recv()
     beside(3, 0).wait_recv()
-    numer[...] = jnp.zeros_like(numer)
-    denom[...] = jnp.zeros_like(denom)
     late = sorted(events)
 
     @pl.loop(0, S // 4)
@@ -348,15 +335,11 @@
 
         for i in range(4):
             total[4 * t + i] = times_right(4 * t + i, 0, SPLIT)
-            psi = psi_of(4 * t + i)
-            denom[...] += jnp.sum((psi * psi).reshape(BS // 8, 8, NV * BS), axis=0)
 
     for at in sorted(events):
         run(at)
     beside(1, FIRST).wait_recv()
     beside(3, FIRST).wait_recv()
-    tail_beside(1).wait_recv()
-    tail_beside(3).wait_recv()
 
     wide_row = jnp.full((1, NV * BS), live, jnp.int32)
     row_live = lax.rem(lax.broadcasted_iota(jnp.int32, (1, NV * BS), 1), BS) < wide_row
@@ -463,8 +446,8 @@
             pltpu.VMEM((8, NV * BS), F32),
             pltpu.VMEM((n_blk, 8, BS), F32),
             dma((7,)),
-            dma((NEAR + 3, CHUNKS + 1)),
-            dma((NEAR + 3, CHUNKS + 1)),
+            dma((NEAR + 3, CHUNKS)),
+            dma((NEAR + 3, CHUNKS)),
             dma((n_blk,)),
             dma((n_blk,)),
             pltpu.SemaphoreType.REGULAR((3,)),

time: 47.9 us -> 47 us (0.981)
  Pallas kernels: 46.3 us -> 45.4 us
    pallas_call x1, Pallas kernels: 43.6 us -> 42.8 us  [local(): pl.pallas_call(lambda *refs: apply_kernel(n_blk, *refs), out_shape=(pltpu...]
where the time goes in v3:
time: 47 us; the launch traced here: 46.9 us
  Pallas kernels  45.4 us (97%)
  between operations  1.45 us (3%)
    pallas_call x1, Pallas kernels, local(): pl.pallas_call(lambda *refs: apply_kernel(n_blk, *refs), out_shape=(pltpu...  42.8 us
    pallas_call x1, Pallas kernels, local(): pl.pallas_call(residual_kernel, out_shape=(jax.ShapeDtypeStruct((NV * S,...  2.67 us

profile of v3, /device:TPU:1, one launch (start us, length us, event | category | flops | bytes accessed | tf_op | source)
XLA Modules:
  0.0 46.9 jit_solution(3508297488423323087)
XLA Ops:
  1.3 42.8 %shard_map.86 = (f32[64,128,128]{2,1,0:T(8,128)S(1)}, bf16[64,128,128]{2,1,0:T(8,128)(2,1)S(1)}, f32[4,128]{1,0:T(4,128)S(1)}) custom-call(bf16[64,128,128]{2,1,0:T(8,128)(2,1)} %bitcast.5, bf16[14,128,128]{2,1,0:T(8,128)(2,1)} %bitcast.6, bf16[14,128,128]{2,1,0:T(8,128)(2,1)} %bitcast.7, bf16[14,16,16]{2,1,0:T(8,128)(2,1)} %refs_3_.1, ...), custom_call_target="tpu_custom_call" | custom-call | tf_op jit(solution)/shard_map/pallas_call | solution.py:416
  44.0 2.7 %shard_map.87 = (f32[64,128,128]{2,1,0:T(8,128)}, f32[1,4]{1,0:T(1,128)}) custom-call(f32[64,128,128]{2,1,0:T(8,128)S(1)} %get-tuple-element.7.hpsi_ref, bf16[64,128,128]{2,1,0:T(8,128)(2,1)S(1)} %get-tuple-element.8.psi_ref, f32[4,128]{1,0:T(4,128)S(1)} %get-tuple-element.9.theta_ref), custom_call_target="tpu_custom_call" | custom-call | tf_op jit(solution)/shard_map/pallas_call | solution.py:467

commit v4 on v3

--- a/solution.py
+++ b/solution.py
@@ -324,17 +324,17 @@
     beside(3, 0).wait_recv()
     late = sorted(events)
 
-    @pl.loop(0, S // 4)
+    @pl.loop(0, S // 8)
     def _(t):
         for at in late:
             if at - steps < 8:
 
-                @pl.when(t == (at - steps) // 2)
+                @pl.when(t == (at - steps) // 4)
                 def _(at=at):
                     run(at)
 
-        for i in range(4):
-            total[4 * t + i] = times_right(4 * t + i, 0, SPLIT)
+        for i in range(8):
+            total[8 * t + i] = times_right(8 * t + i, 0, SPLIT)
 
     for at in sorted(events):
         run(at)
@@ -345,10 +345,10 @@
     row_live = lax.rem(lax.broadcasted_iota(jnp.int32, (1, NV * BS), 1), BS) < wide_row
     column = lax.broadcasted_iota(jnp.int32, (BS, BS), 0).astype(F32)
 
-    @pl.loop(0, S // 4)
+    @pl.loop(0, S // 8)
     def _(t):
-        for i in range(4):
-            at = 4 * t + i
+        for i in range(8):
+            at = 8 * t + i
             product = total[at] + times_right(at, SPLIT, W)
             sector = offsets[0, at]
             bound = near_b[sector, pl.ds(REST, SUB), :][:1].astype(F32)

time: 47 us -> 46.5 us (0.989)
  Pallas kernels: 45.4 us -> 44.9 us
    pallas_call x1, Pallas kernels: 42.8 us -> 42.3 us  [local(): pl.pallas_call(lambda *refs: apply_kernel(n_blk, *refs), out_shape=(pltpu...]
where the time goes in v4:
time: 46.5 us; the launch traced here: 46.4 us
  Pallas kernels  44.9 us (97%)
  between operations  1.45 us (3%)
    pallas_call x1, Pallas kernels, local(): pl.pallas_call(lambda *refs: apply_kernel(n_blk, *refs), out_shape=(pltpu...  42.3 us
    pallas_call x1, Pallas kernels, local(): pl.pallas_call(residual_kernel, out_shape=(jax.ShapeDtypeStruct((NV * S,...  2.67 us

profile of v4, /device:TPU:1, one launch (start us, length us, event | category | flops | bytes accessed | tf_op | source)
XLA Modules:
  0.0 46.4 jit_solution(8402783859844972106)
XLA Ops:
  1.3 42.3 %shard_map.86 = (f32[64,128,128]{2,1,0:T(8,128)S(1)}, bf16[64,128,128]{2,1,0:T(8,128)(2,1)S(1)}, f32[4,128]{1,0:T(4,128)S(1)}) custom-call(bf16[64,128,128]{2,1,0:T(8,128)(2,1)} %bitcast.5, bf16[14,128,128]{2,1,0:T(8,128)(2,1)} %bitcast.6, bf16[14,128,128]{2,1,0:T(8,128)(2,1)} %bitcast.7, bf16[14,16,16]{2,1,0:T(8,128)(2,1)} %refs_3_.1, ...), custom_call_target="tpu_custom_call" | custom-call | tf_op jit(solution)/shard_map/pallas_call | solution.py:416
  43.5 2.7 %shard_map.87 = (f32[64,128,128]{2,1,0:T(8,128)}, f32[1,4]{1,0:T(1,128)}) custom-call(f32[64,128,128]{2,1,0:T(8,128)S(1)} %get-tuple-element.7.hpsi_ref, bf16[64,128,128]{2,1,0:T(8,128)(2,1)S(1)} %get-tuple-element.8.psi_ref, f32[4,128]{1,0:T(4,128)S(1)} %get-tuple-element.9.theta_ref), custom_call_target="tpu_custom_call" | custom-call | tf_op jit(solution)/shard_map/pallas_call | solution.py:467
